TPU v7x, 256 devices: a whole 4x4x8 slice. The times are simulated.
256 devices in a mesh: ctx: 32 (over y, z), head: 8 (over x, core).
Axes of the slice: x: 4, y: 4, z: 8, core: 2. Of those that a mesh axis runs over, the one named last changes fastest.
Arguments:
- queries: bfloat16 [32768, 2048], P('ctx', 'head'), may hold values from -6 to 6
- key_vectors: bfloat16 [32768, 2048], P('ctx', 'head'), may hold values from -6 to 6
- value_vectors: bfloat16 [32768, 2048], P('ctx', 'head'), may hold values from -60 to 60
- write_rates: float32 [32768, 16], P('ctx', 'head'), may hold values from 0 to 1
- doc_lengths: int32 [32], replicated, may hold values from 1 to 16384, 32768 in all
- norm_gain: float32 [2048], P('head'), may hold values from 0.5 to 1.5
Outputs:
- normed: bfloat16 [32768, 2048], P('ctx', 'head')
All inputs are finite; a program needn't handle non-finite values.
Results may differ from a plain program's by a relative error of at most 0.0014.
Values sent between devices are 32-bit elements; how exact they have to be, the bound alone decides.
A program may use at most 64 MiB of HBM per device.

v0:
```python
import jax
import jax.numpy as jnp
from jax import lax
from jax.sharding import PartitionSpec as P

BLOCK = 128
highest = lax.Precision.HIGHEST
epsilon = 1e-06


def entering(part, axis, combine, identity):
    place = lax.axis_index(axis)
    gathered = jax.tree.map(lambda a: lax.all_gather(a, axis), part)
    state = jax.tree.map(lambda a, e: jnp.zeros_like(a) + jnp.asarray(e, a.dtype), part, identity)

    def one(lap, state):
        return combine(
            state, jax.tree.map(lambda a: lax.dynamic_index_in_dim(a, lap, 0, False), gathered)
        )

    return lax.fori_loop(0, place, one, state)


def normalize(rows):
    return rows * lax.rsqrt(jnp.sum(rows * rows, axis=-1, keepdims=True) + epsilon)


def document_ids(doc_lengths, positions):
    ends = jnp.cumsum(doc_lengths, dtype=jnp.int32)
    begins = ends - doc_lengths
    return jnp.sum((begins[None, :] <= positions[:, None]).astype(jnp.int32), axis=1) - 1


def combine_pairs(earlier, later):
    mul_early, add_early = earlier
    mul_late, add_late = later
    product = jnp.einsum("hij,hjk->hik", mul_late, mul_early, precision=highest)
    shifted = jnp.einsum("hij,hjk->hik", mul_late, add_early, precision=highest) + add_late
    return (product, shifted)


def local(queries, key_vectors, value_vectors, write_rates, doc_lengths, norm_gain):
    tok_dev = queries.shape[0]
    head_count = write_rates.shape[1]
    head_dim = queries.shape[1] // head_count
    block_count = tok_dev // BLOCK

    def split_heads(matrix):
        return (
            matrix.astype(jnp.float32)
            .reshape(block_count, BLOCK, head_count, head_dim)
            .transpose(0, 2, 1, 3)
        )

    query_blocks = normalize(split_heads(queries))
    key_blocks = normalize(split_heads(key_vectors))
    value_blocks = split_heads(value_vectors)
    rate_blocks = write_rates.reshape(block_count, BLOCK, head_count).transpose(0, 2, 1)
    offset = lax.axis_index("ctx") * tok_dev
    positions = offset + jnp.arange(tok_dev, dtype=jnp.int32)
    doc_here = document_ids(doc_lengths, positions).reshape(block_count, BLOCK)
    block_begin = offset + jnp.arange(block_count, dtype=jnp.int32) * BLOCK - 1
    doc_before = document_ids(doc_lengths, block_begin)
    carry_mask = (doc_here == doc_before[:, None]).astype(jnp.float32)
    last_mask = (doc_here == doc_here[:, -1:]).astype(jnp.float32)
    same_doc = doc_here[:, None, :, None] == doc_here[:, None, None, :]
    rows_index = jnp.arange(BLOCK)
    lower_strict = rows_index[:, None] > rows_index[None, :]
    lower_incl = rows_index[:, None] >= rows_index[None, :]
    key_gram = jnp.einsum("nhcd,nhed->nhce", key_blocks, key_blocks, precision=highest)
    coupling = jnp.where(lower_strict & same_doc, rate_blocks[..., :, None] * key_gram, 0.0)
    system = coupling + jnp.eye(BLOCK, dtype=jnp.float32)
    stacked = jnp.concatenate([key_blocks, value_blocks], axis=-1) * rate_blocks[..., None]
    solved = jax.scipy.linalg.solve_triangular(system, stacked, lower=True, unit_diagonal=True)
    wy_keys = solved[..., :head_dim]
    wy_values = solved[..., head_dim:]
    scores = jnp.einsum("nhcd,nhed->nhce", query_blocks, key_blocks, precision=highest)
    scores = jnp.where(lower_incl & same_doc, scores, 0.0)
    carried_keys = wy_keys * carry_mask[:, None, :, None]
    last_keys = key_blocks * last_mask[:, None, :, None]
    carried_queries = query_blocks * carry_mask[:, None, :, None]
    carry_last = carry_mask[:, -1]
    identity_mat = jnp.broadcast_to(
        jnp.eye(head_dim, dtype=jnp.float32), (head_count, head_dim, head_dim)
    )
    zero_state = jnp.zeros((head_count, head_dim, head_dim), jnp.float32)
    step_mul = carry_last[:, None, None, None] * identity_mat[None] - jnp.einsum(
        "nhcd,nhce->nhde", last_keys, carried_keys, precision=highest
    )
    step_add = jnp.einsum("nhcd,nhce->nhde", last_keys, wy_values, precision=highest)

    def fold_pairs(pair, block_pair):
        return (combine_pairs(pair, block_pair), None)

    (dev_mul, dev_add), _ = lax.scan(fold_pairs, (identity_mat, zero_state), (step_mul, step_add))
    _, entry_state = entering((dev_mul, dev_add), "ctx", combine_pairs, (identity_mat, zero_state))

    def run_one(state, block):
        query_now, score_now, carried_now, value_now, last_now, keep_now = block
        updated = value_now - jnp.einsum("hcd,hde->hce", carried_now, state, precision=highest)
        output = jnp.einsum("hcd,hde->hce", query_now, state, precision=highest)
        output = output + jnp.einsum("hce,hed->hcd", score_now, updated, precision=highest)
        state = keep_now * state + jnp.einsum("hcd,hce->hde", last_now, updated, precision=highest)
        return (state, output)

    _, outputs = lax.scan(
        run_one,
        entry_state,
        (carried_queries, scores, carried_keys, wy_values, last_keys, carry_last),
    )
    outputs = outputs.transpose(0, 2, 1, 3).reshape(tok_dev, head_count * head_dim)
    local_squares = jnp.sum(outputs * outputs, axis=1)
    total_squares = lax.psum(local_squares, "head")
    width_all = head_count * head_dim * lax.axis_size("head")
    scale = lax.rsqrt(total_squares / width_all + epsilon)
    return (outputs * scale[:, None] * norm_gain[None, :]).astype(jnp.bfloat16)


def solution(mesh):
    placed = (
        P("ctx", "head"),
        P("ctx", "head"),
        P("ctx", "head"),
        P("ctx", "head"),
        P(),
        P("head"),
    )
    return jax.shard_map(
        local, mesh=mesh, in_specs=placed, out_specs=P("ctx", "head"), check_vma=False
    )
```

profile of v0, /device:TPU:249, one launch (start us, length us, event | category | flops | bytes accessed | tf_op | source)
XLA Modules:
  0.0 490.3 jit_solution(16350187449445751479)
XLA Ops:
  7.2 1.3 copy.94
  12.1 1.5 reshape.194
  16.2 1.6 copy.91
  17.8 1.6 compare_and_fusion
  19.4 4.1 fusion.35
  23.5 158.6 %custom-call.4 = f32[8,2,1,128,128]{3,4,2,1,0:T(8,128)} custom-call(f32[8,2,1,128,128]{4,3,2,1,0:T(8,128)} %fusion.35), custom_call_target="InvertDiagBlocksLowerTriangular" | custom-call | tf_op jit(solution)/shard_map/jit(_solve_triangular)/vmap(vmap())/triangular_solve | solution.py:74
  182.1 2.5 reshape.193
  184.7 2.5 copy.108
  187.2 1.8 maximum_multiply_fusion
  189.1 2.3 fusion.29
  191.4 2.3 fusion.47
  193.7 1.9 fusion.51
  196.6 2.3 convolution_subtract_fusion.1
  199.0 19.9 %while.42 = (s32[]{:T(128)}, f32[2,128,128]{2,1,0:T(8,128)S(1)}, f32[2,128,128]{2,1,0:T(8,128)S(1)}, f32[8,2,128,128]{3,2,1,0:T(8,128)}, f32[8,2,128,128]{3,2,1,0:T(8,128)}) while((s32[]{:T(128)}, f32[2,128,128]{2,1,0:T(8,128)S(1)}, f32[2,128,128]{2,1,0:T(8,128)S(1)}, f32[8,2,128,128]{3,2,1,0:T(8,128)}, ...), condition=%wide.region_5.6_spmd.clone.clone, body=%wide.region_4.5_spmd.clone.sunk.clone | while | flops 100728832 | bytes 1443410 | solution.py:95
  221.4 3.3 convolution_select_fusion
  224.8 70.8 %all-gather.7.cloned.1.call-done = f32[64,128,128]{2,1,0:T(8,128)} async-done(((f32[2,128,128]{2,1,0:T(8,128)}), f32[64,128,128]{2,1,0:T(8,128)}) %all-gather.7.cloned.1.call-update) | async-done | bytes 4194320 | tf_op jit(solution)/shard_map/all_gather | solution.py:13
  295.5 81.7 %all-gather.5.cloned.1.call-done = f32[64,128,128]{2,1,0:T(8,128)} async-done(((f32[2,128,128]{2,1,0:T(8,128)}), f32[64,128,128]{2,1,0:T(8,128)}) %all-gather.5.cloned.1.call-update) | async-done | bytes 4194320 | tf_op jit(solution)/shard_map/all_gather | solution.py:13
  377.2 39.9 %while.40 = (s32[]{:T(128)}, f32[2,128,128]{2,1,0:T(8,128)S(1)}, s32[]{:T(128)}, f32[32,2,128,128]{3,2,1,0:T(8,128)}, f32[32,2,128,128]{3,2,1,0:T(8,128)}) while((s32[]{:T(128)}, f32[2,128,128]{2,1,0:T(8,128)S(1)}, s32[]{:T(128)}, f32[32,2,128,128]{3,2,1,0:T(8,128)}, f32[32,2,128,128]{3,2,1,0:T(8,128)}) %tuple.87), condition=%wide.region_7.8_spmd.clone, body=%wide.region_6.7_spmd.sunk.clone | while | flops 50364420 | bytes 787559 | solution.py:21
  388.9 1.2 convolution_add_fusion.10
  404.3 1.2 convolution_add_fusion.10
  409.4 1.2 convolution_add_fusion.10
  414.6 1.2 convolution_add_fusion.10
  417.1 48.3 %while.41 = (s32[]{:T(128)}, f32[2,128,128]{2,1,0:T(8,128)S(1)}, f32[8,2,128,128]{3,2,1,0:T(8,128)S(1)}, f32[8]{0:T(128)S(1)}, f32[8,2,128,128]{2,3,1,0:T(8,128)...) while((s32[]{:T(128)}, f32[2,128,128]{2,1,0:T(8,128)S(1)}, ...), condition=%wide.region_10.11_spmd.clone, body=%wide.region_9.10_spmd.sunk.clone | while | flops 201457664 | bytes 1968761 | solution.py:106
  420.1 1.8 convolution_add_fusion.11
  426.2 1.8 convolution_add_fusion.11
  432.2 1.8 convolution_add_fusion.11
  438.3 1.8 convolution_add_fusion.11
  444.3 1.8 convolution_add_fusion.11
  450.4 1.8 convolution_add_fusion.11
  456.4 1.8 convolution_add_fusion.11
  462.4 1.8 convolution_add_fusion.11
  465.7 15.9 %psum.7 = f32[1024]{0:T(1024)S(1)} all-reduce(f32[1024]{0:T(1024)S(1)} %bitcast.145), channel_id=1, replica_groups=mesh['ctx'=32,'head'=8] {'head'}, use_global_device_ids=true, to_apply=%region_12.13 | all-reduce | flops 1024 | bytes 8192 | tf_op jit(solution)/shard_map/psum | solution.py:113
  (178 shorter events, 99.1 us)
Async XLA Ops:
  6.5 7.5 %copy-start.4 = (bf16[1024,256]{1,0:T(8,128)(2,1)S(1)}, bf16[1024,256]{1,0:T(8,128)(2,1)}, u32[]{:S(2)}) copy-start(bf16[1024,256]{1,0:T(8,128)(2,1)} %param.13) | copy-start | bytes 1572868
  6.5 289.0 %all-gather.7.cloned.1.call-start = ((), (), s32[]{:S(2)}) async-start(), calls=%async_computation.1 | async-start | bytes 4325376 | tf_op jit(solution)/shard_map/all_gather | solution.py:13
  23.5 163.7 %copy-start.6 = (f32[8,2,128]{2,0,1:T(8,128)S(1)}, f32[8,2,128]{2,0,1:T(8,128)}, u32[]{:S(2)}) copy-start(f32[8,2,128]{2,0,1:T(8,128)} %copy.94) | copy-start | bytes 24580
  187.2 1.9 copy-start.3
  193.7 2.9 copy-start.7
  195.6 1.0 copy-start
  218.8 0.7 copy-start.2
  218.8 0.7 copy-start.1
  218.9 2.6 copy-start.5
  219.5 157.7 %all-gather.5.cloned.1.call-start = ((), (), s32[]{:S(2)}) async-start(), calls=%async_computation | async-start | bytes 4325376 | tf_op jit(solution)/shard_map/all_gather | solution.py:13
  465.5 17.0 %copy-start.8 = (f32[256]{0:T(256)S(1)}, f32[256]{0:T(256)}, u32[]{:S(2)}) copy-start(f32[256]{0:T(256)} %param.17) | copy-start | bytes 3076
Sparse Core Ops, SparseCore 0:
  219.6 75.8 all-gather.6
  298.1 79.0 all-gather.4
where the time goes:
time: 492 us; the launch traced here: 490 us
  other arithmetic  169 us (34%)
  waiting for transfers between devices  153 us (31%)
  matrix products  115 us (23%)
  local copies, waits for them, and re-layouts  21 us (4%)
  blocking collectives  15.9 us (3%)
  between operations  13.6 us (3%)
    another operation x4, other arithmetic, local(): jax.scipy.linalg.solve_triangular(system, stacked, lower=True, unit_diago...  159 us
    all_gather x2, waiting for transfers between devices, entering(): gathered = jax.tree.map(lambda a: lax.all_gather(a, axis), part)  152 us
    dot_general x39, matrix products, combine_pairs(): jnp.einsum('hij,hjk->hik', mul_late, add_early, precision=highest)  48.4 us
    psum x1, blocking collectives, local(): total_squares = lax.psum(local_squares, 'head')  15.9 us
    dot_general x8, matrix products, run_one(): jnp.einsum('hcd,hce->hde', last_now, updated, precision=highest)  14.6 us
    dot_general x8, matrix products, run_one(): jnp.einsum('hcd,hde->hce', carried_now, state, precision=highest)  9.86 us
  transfers between devices with their start and end apart: 2, of which 2 were waited for; matrix products, arithmetic and copies ran while one was open for 1% of the time, Pallas kernels for 0%

commit v1 on v0

--- a/solution.py
+++ b/solution.py
@@ -1,3 +1,4 @@
+import functools
 import jax
 import jax.numpy as jnp
 from jax import lax
@@ -6,6 +7,14 @@
 BLOCK = 128
 highest = lax.Precision.HIGHEST
 epsilon = 1e-06
+
+
+def remake_ranges(mine, axis_name):
+    extra = lax.all_gather(mine, axis_name)
+    return jnp.sum(extra, 0)
+
+
+_measure_task = functools.partial(remake_ranges, axis_name="head")
 
 
 def entering(part, axis, combine, identity):
@@ -110,7 +119,7 @@
     )
     outputs = outputs.transpose(0, 2, 1, 3).reshape(tok_dev, head_count * head_dim)
     local_squares = jnp.sum(outputs * outputs, axis=1)
-    total_squares = lax.psum(local_squares, "head")
+    total_squares = _measure_task(local_squares)
     width_all = head_count * head_dim * lax.axis_size("head")
     scale = lax.rsqrt(total_squares / width_all + epsilon)
     return (outputs * scale[:, None] * norm_gain[None, :]).astype(jnp.bfloat16)

time: 492 us -> 494 us (level)
    all_gather x0 -> x1, blocking collectives: none -> 17 us  [remake_ranges(): extra = lax.all_gather(mine, axis_name)]
    psum x1 -> x0, blocking collectives: 15.9 us -> none  [local(): total_squares = lax.psum(local_squares, 'head')]
where the time goes in v1:
time: 494 us; the launch traced here: 492 us
  other arithmetic  169 us (34%)
  waiting for transfers between devices  153 us (31%)
  matrix products  115 us (23%)
  local copies, waits for them, and re-layouts  21 us (4%)
  blocking collectives  17 us (3%)
  between operations  13.6 us (3%)
    another operation x4, other arithmetic, local(): jax.scipy.linalg.solve_triangular(system, stacked, lower=True, unit_diago...  159 us
    all_gather x2, waiting for transfers between devices, entering(): gathered = jax.tree.map(lambda a: lax.all_gather(a, axis), part)  152 us
    dot_general x39, matrix products, combine_pairs(): jnp.einsum('hij,hjk->hik', mul_late, add_early, precision=highest)  48.4 us
    all_gather x1, blocking collectives, remake_ranges(): extra = lax.all_gather(mine, axis_name)  17 us
    dot_general x8, matrix products, run_one(): jnp.einsum('hcd,hce->hde', last_now, updated, precision=highest)  14.6 us
  transfers between devices with their start and end apart: 2, of which 2 were waited for; matrix products, arithmetic and copies ran while one was open for 1% of the time, Pallas kernels for 0%

profile of v1, /device:TPU:249, one launch (start us, length us, event | category | flops | bytes accessed | tf_op | source)
XLA Modules:
  0.0 491.7 jit_solution(11008018842772264741)
XLA Ops:
  7.2 1.3 copy.94
  12.1 1.5 reshape.202
  16.2 1.6 copy.91
  17.8 1.6 compare_and_fusion
  19.4 4.1 fusion.35
  23.5 158.6 %custom-call.4 = f32[8,2,1,128,128]{3,4,2,1,0:T(8,128)} custom-call(f32[8,2,1,128,128]{4,3,2,1,0:T(8,128)} %fusion.35), custom_call_target="InvertDiagBlocksLowerTriangular" | custom-call | tf_op jit(solution)/shard_map/jit(_solve_triangular)/vmap(vmap())/triangular_solve | solution.py:83
  182.1 2.5 reshape.201
  184.7 2.5 copy.108
  187.2 1.8 maximum_multiply_fusion
  189.1 2.3 fusion.29
  191.4 2.3 fusion.47
  193.7 1.9 fusion.51
  196.6 2.3 convolution_subtract_fusion.1
  199.0 19.9 %while.42 = (s32[]{:T(128)}, f32[2,128,128]{2,1,0:T(8,128)S(1)}, f32[2,128,128]{2,1,0:T(8,128)S(1)}, f32[8,2,128,128]{3,2,1,0:T(8,128)}, f32[8,2,128,128]{3,2,1,0:T(8,128)}) while((s32[]{:T(128)}, f32[2,128,128]{2,1,0:T(8,128)S(1)}, f32[2,128,128]{2,1,0:T(8,128)S(1)}, f32[8,2,128,128]{3,2,1,0:T(8,128)}, ...), condition=%wide.region_5.6_spmd.clone.clone, body=%wide.region_4.5_spmd.clone.sunk.clone | while | flops 100728832 | bytes 1443410 | solution.py:104
  221.4 3.3 convolution_select_fusion
  224.8 70.8 %all-gather.8.cloned.1.call-done = f32[64,128,128]{2,1,0:T(8,128)} async-done(((f32[2,128,128]{2,1,0:T(8,128)}), f32[64,128,128]{2,1,0:T(8,128)}) %all-gather.8.cloned.1.call-update) | async-done | bytes 4194320 | tf_op jit(solution)/shard_map/all_gather | solution.py:22
  295.5 81.7 %all-gather.6.cloned.1.call-done = f32[64,128,128]{2,1,0:T(8,128)} async-done(((f32[2,128,128]{2,1,0:T(8,128)}), f32[64,128,128]{2,1,0:T(8,128)}) %all-gather.6.cloned.1.call-update) | async-done | bytes 4194320 | tf_op jit(solution)/shard_map/all_gather | solution.py:22
  377.2 39.9 %while.40 = (s32[]{:T(128)}, f32[2,128,128]{2,1,0:T(8,128)S(1)}, s32[]{:T(128)}, f32[32,2,128,128]{3,2,1,0:T(8,128)}, f32[32,2,128,128]{3,2,1,0:T(8,128)}) while((s32[]{:T(128)}, f32[2,128,128]{2,1,0:T(8,128)S(1)}, s32[]{:T(128)}, f32[32,2,128,128]{3,2,1,0:T(8,128)}, f32[32,2,128,128]{3,2,1,0:T(8,128)}) %tuple.87), condition=%wide.region_7.8_spmd.clone, body=%wide.region_6.7_spmd.sunk.clone | while | flops 50364420 | bytes 787559 | solution.py:30
  388.9 1.2 convolution_add_fusion.10
  404.3 1.2 convolution_add_fusion.10
  409.4 1.2 convolution_add_fusion.10
  414.6 1.2 convolution_add_fusion.10
  417.1 48.6 %while.41 = (s32[]{:T(128)}, f32[2,128,128]{2,1,0:T(8,128)S(1)}, f32[8,2,128,128]{3,2,1,0:T(8,128)S(1)}, f32[8]{0:T(128)S(1)}, f32[8,2,128,128]{2,3,1,0:T(8,128)...) while((s32[]{:T(128)}, f32[2,128,128]{2,1,0:T(8,128)S(1)}, ...), condition=%wide.region_10.11_spmd.clone, body=%wide.region_9.10_spmd.sunk.clone | while | flops 201457664 | bytes 1968761 | solution.py:115
  420.4 1.8 convolution_add_fusion.11
  426.4 1.8 convolution_add_fusion.11
  432.4 1.8 convolution_add_fusion.11
  438.5 1.8 convolution_add_fusion.11
  444.5 1.8 convolution_add_fusion.11
  450.6 1.8 convolution_add_fusion.11
  456.6 1.8 convolution_add_fusion.11
  462.7 1.8 convolution_add_fusion.11
  465.9 17.0 %all-gather.2 = f32[8,1,1024]{2,1,0:T(1,128)S(1)} all-gather(f32[1,1,1024]{2,1,0:T(1,128)S(1)} %bitcast.145), channel_id=1, replica_groups=mesh['ctx'=32,'head'=8] {'head'}, dimensions={0}, use_global_device_ids=true | all-gather | bytes 36864 | tf_op jit(solution)/shard_map/all_gather | solution.py:13
  (179 shorter events, 99.1 us)
Async XLA Ops:
  6.5 7.5 %copy-start.4 = (bf16[1024,256]{1,0:T(8,128)(2,1)S(1)}, bf16[1024,256]{1,0:T(8,128)(2,1)}, u32[]{:S(2)}) copy-start(bf16[1024,256]{1,0:T(8,128)(2,1)} %param.13) | copy-start | bytes 1572868
  6.5 289.0 %all-gather.8.cloned.1.call-start = ((), (), s32[]{:S(2)}) async-start(), calls=%async_computation.1 | async-start | bytes 4325376 | tf_op jit(solution)/shard_map/all_gather | solution.py:22
  23.5 163.7 %copy-start.6 = (f32[8,2,128]{2,0,1:T(8,128)S(1)}, f32[8,2,128]{2,0,1:T(8,128)}, u32[]{:S(2)}) copy-start(f32[8,2,128]{2,0,1:T(8,128)} %copy.94) | copy-start | bytes 24580
  187.2 1.9 copy-start.3
  193.7 2.9 copy-start.7
  195.6 1.0 copy-start
  218.8 0.7 copy-start.2
  218.8 0.7 copy-start.1
  218.9 2.6 copy-start.5
  219.5 157.7 %all-gather.6.cloned.1.call-start = ((), (), s32[]{:S(2)}) async-start(), calls=%async_computation | async-start | bytes 4325376 | tf_op jit(solution)/shard_map/all_gather | solution.py:22
  465.7 18.1 %copy-start.8 = (f32[256]{0:T(256)S(1)}, f32[256]{0:T(256)}, u32[]{:S(2)}) copy-start(f32[256]{0:T(256)} %param.17) | copy-start | bytes 3076
Sparse Core Ops, SparseCore 0:
  219.6 75.8 all-gather.7
  298.1 79.0 all-gather.5
